TPU v7x, 512 devices: a whole 4x4x16 slice. The times are simulated.
512 devices in a mesh: dp: 8 (over x, core), ctx: 64 (over z, y).
Axes of the slice: x: 4, y: 4, z: 16, core: 2. Of those that a mesh axis runs over, the one named last changes fastest.
Arguments:
- tokens: bfloat16 [8, 8192, 4096], P('dp', 'ctx'), may hold values from -8 to 8
- queries: bfloat16 [8, 8192, 4096], P('dp', 'ctx'), may hold values from -170 to 170
- key_weight: bfloat16 [4096, 512], P(('dp', 'ctx')), may hold values from -0.09375 to 0.09375
- value_weight: bfloat16 [4096, 512], P(('dp', 'ctx')), may hold values from -0.09375 to 0.09375
- bounds: int32 [3, 8, 8192], P(None, 'dp', 'ctx'), may hold values from 0 to 8191, as said below
Outputs:
- context: bfloat16 [8, 8192, 4096], P('dp', 'ctx')
Inputs may be any that keep to these rules, and one draw needn't show every extreme that they name: Pairs are runs of consecutive tokens that cover each pack. For a token t, bounds[0] is the first position of its pair, bounds[1] the first of its chosen reply, bounds[2] the first of its rejected reply, the same for every token of the pair, with bounds[0] < bounds[1] < bounds[2] <= the pair's last position. A pair has at most 512 tokens, and every pack holds a pair of exactly 512.
All inputs are finite; a program needn't handle non-finite values.
Results may differ from a plain program's by a relative error of at most 0.011.
Values may be sent and summed in bfloat16 or wider, within the bound.
No kernel may reach another device: no remote copies, remote signals or barrier semaphores. Data moves between devices by JAX's collectives and lax.ppermute only.
A program may use at most 64 MiB of HBM per device.

v0:
```python
import math

import jax
import jax.numpy as jnp
from jax import lax
from jax.sharding import PartitionSpec as P

HD = 128


NEG_FILL = -1e30


def shifted(block, axis, distance):
    devices = range(lax.axis_size(axis))
    route = [(i - distance, i) for i in devices if i - distance in devices]
    return lax.ppermute(block, axis, route)


def frequencies(head_size):
    halves = jnp.arange(head_size // 2, dtype=jnp.float32)
    base_rate = 500000.0 ** (-2.0 * halves / head_size)
    wavelength = 2.0 * math.pi / base_rate
    mixing = (8192.0 / wavelength - 1.0) / 3.0
    middle = (1.0 - mixing) * base_rate / 8.0 + mixing * base_rate
    return jnp.where(
        wavelength < 2048.0, base_rate, jnp.where(wavelength > 8192.0, base_rate / 8.0, middle)
    )


def positions(limits, places):
    return jnp.where(
        places < limits[2], places - limits[0], places - limits[0] - (limits[2] - limits[1])
    )


def rotate(vectors, offsets, rates):
    angles = offsets.astype(jnp.float32)[:, None] * rates[None, :]
    cos_part = jnp.cos(angles)[:, None, :]
    sin_part = jnp.sin(angles)[:, None, :]
    half_size = vectors.shape[-1] // 2
    lower_half = vectors[..., :half_size]
    upper_half = vectors[..., half_size:]
    return jnp.concatenate(
        [
            lower_half * cos_part - upper_half * sin_part,
            upper_half * cos_part + lower_half * sin_part,
        ],
        axis=-1,
    )


def shards(tokens, queries, key_weight, value_weight, bounds):
    local_len = tokens.shape[1]
    kv_width = key_weight.shape[1]
    kv_heads = kv_width // HD
    head_count = queries.shape[2] // HD
    group_size = head_count // kv_heads
    head_scale = HD ** (-0.5)
    pair_span = min(4, lax.axis_size("ctx") // 4)
    token_rows = tokens[0]
    keys_raw = jnp.dot(
        token_rows,
        lax.all_gather(key_weight, ("dp", "ctx"), axis=0, tiled=True),
        preferred_element_type=jnp.float32,
    )
    values_raw = jnp.dot(
        token_rows,
        lax.all_gather(value_weight, ("dp", "ctx"), axis=0, tiled=True),
        preferred_element_type=jnp.float32,
    )
    my_index = lax.axis_index("ctx")
    places = my_index * local_len + jnp.arange(local_len, dtype=jnp.int32)
    limits = bounds[:, 0, :]
    offsets = positions(limits, places)
    rates = frequencies(HD)
    own_keys = rotate(keys_raw.reshape(local_len, kv_heads, HD), offsets, rates).astype(
        jnp.bfloat16
    )
    own_values = values_raw.astype(jnp.bfloat16).reshape(local_len, kv_heads, HD)
    turned = rotate(
        queries[0].astype(jnp.float32).reshape(local_len, head_count, HD), offsets, rates
    )
    turned = turned.astype(jnp.bfloat16).reshape(local_len, kv_heads, group_size, HD)
    begin_at = limits[0]
    chosen_at = limits[1]
    reject_at = limits[2]
    later_part = places >= reject_at

    def update(state, key_block, value_block, key_base):
        running, denominator, accumulated = state
        key_index = key_base + jnp.arange(local_len, dtype=jnp.int32)
        excluded = (
            later_part[:, None]
            & (key_index[None, :] >= chosen_at[:, None])
            & (key_index[None, :] < reject_at[:, None])
        )
        visible = (
            (key_index[None, :] >= begin_at[:, None])
            & (key_index[None, :] <= places[:, None])
            & jnp.logical_not(excluded)
        )
        scores = (
            jnp.einsum("qhgd,khd->hgqk", turned, key_block, preferred_element_type=jnp.float32)
            * head_scale
        )
        masked = jnp.where(visible, scores, NEG_FILL)
        highest = jnp.maximum(running, jnp.max(masked, axis=-1))
        weights = jnp.exp(masked - highest[..., None])
        fading = jnp.exp(running - highest)
        denominator = denominator * fading + jnp.sum(weights, axis=-1)
        product = jnp.einsum(
            "hgqk,khd->hgqd",
            weights.astype(jnp.bfloat16),
            value_block,
            preferred_element_type=jnp.float32,
        )
        accumulated = accumulated * fading[..., None] + product
        return (highest, denominator, accumulated)

    start_state = (
        jnp.full((kv_heads, group_size, local_len), NEG_FILL, jnp.float32),
        jnp.zeros((kv_heads, group_size, local_len), jnp.float32),
        jnp.zeros((kv_heads, group_size, local_len, HD), jnp.float32),
    )
    state = update(start_state, own_keys, own_values, my_index * local_len)
    moving = (own_keys, own_values)
    for distance in range(1, pair_span + 1):
        moving = shifted((moving[0], moving[1]), "ctx", 1)
        consider_key_base = (my_index - distance) * local_len
        result = update(state, moving[0], moving[1], consider_key_base)
        state = result
    running, denominator, accumulated = state
    context = accumulated / denominator[..., None]
    context = jnp.transpose(context, (2, 0, 1, 3)).reshape(1, local_len, head_count * HD)
    return context.astype(jnp.bfloat16)


def solution(mesh):
    return jax.shard_map(
        shards,
        mesh=mesh,
        in_specs=(
            P("dp", "ctx", None),
            P("dp", "ctx", None),
            P(("dp", "ctx"), None),
            P(("dp", "ctx"), None),
            P(None, "dp", "ctx"),
        ),
        out_specs=P("dp", "ctx", None),
        check_vma=False,
    )
```

profile of v0, /device:TPU:134, one launch (start us, length us, event | category | flops | bytes accessed | tf_op | source)
XLA Modules:
  0.0 468.8 jit_solution(15253669048578670166)
XLA Ops:
  9.2 1.4 convert_bitcast_fusion
  11.0 0.7 fusion.57
  11.7 2.4 subtract_convert_fusion
  15.1 194.2 %all-gather.3.cloned.1.call-done = bf16[4096,512]{1,0:T(8,128)(2,1)} async-done(((bf16[8,512]{1,0:T(8,128)(2,1)}), bf16[4096,512]{1,0:T(8,128)(2,1)}) %all-gather.3.cloned.1.call-update) | async-done | bytes 4194320 | tf_op jit(solution)/shard_map/all_gather | solution.py:64
  209.3 6.4 %copy.6 = bf16[512,4096]{1,0:T(8,128)(2,1)} copy(bf16[512,4096]{0,1:T(8,128)(2,1)} %bitcast.232) | data formatting | bytes 8388608 | tf_op jit(solution)/shard_map/dot_general | solution.py:62
  215.7 3.4 fusion.25
  219.2 188.2 %all-gather.5.cloned.1.call-done = bf16[4096,512]{1,0:T(8,128)(2,1)} async-done(((bf16[8,512]{1,0:T(8,128)(2,1)}), bf16[4096,512]{1,0:T(8,128)(2,1)}) %all-gather.5.cloned.1.call-update) | async-done | bytes 4194320 | tf_op jit(solution)/shard_map/all_gather | solution.py:69
  407.3 2.9 convolution_convert_fusion
  410.5 3.3 collective-permute-start.1
  413.8 3.4 collective-permute-start
  417.8 3.6 collective-permute-done.1
  421.4 1.9 collective-permute-start.3
  423.3 1.2 collective-permute-done
  424.4 1.9 collective-permute-start.2
  426.9 4.8 %collective-permute-done.3 = bf16[128,4,128]{0,2,1:T(8,128)(2,1)S(1)} collective-permute-done((bf16[128,4,128]{0,2,1:T(8,128)(2,1)S(1)}, bf16[128,4,128]{0,2,1:T(8,128)(2,1)S(1)}, u32[]{:S(2)}, u32[]{:S(2)}) %collective-permute-start.3) | collective-permute-done | bytes 131104 | tf_op jit(solution)/shard_map/ppermute | solution.py:17
  431.7 1.9 collective-permute-start.5
  433.6 1.0 collective-permute-done.2
  434.6 1.9 collective-permute-start.4
  437.0 6.1 %collective-permute-done.5 = bf16[128,4,128]{0,2,1:T(8,128)(2,1)S(1)} collective-permute-done((bf16[128,4,128]{0,2,1:T(8,128)(2,1)S(1)}, bf16[128,4,128]{0,2,1:T(8,128)(2,1)S(1)}, u32[]{:S(2)}, u32[]{:S(2)}) %collective-permute-start.5) | collective-permute-done | bytes 131104 | tf_op jit(solution)/shard_map/ppermute | solution.py:17
  443.1 1.9 collective-permute-start.7
  445.0 2.1 collective-permute-start.6
  447.7 7.6 %collective-permute-done.6 = bf16[128,4,128]{0,2,1:T(8,128)(2,1)S(1)} collective-permute-done((bf16[128,4,128]{0,2,1:T(8,128)(2,1)S(1)}, bf16[128,4,128]{0,2,1:T(8,128)(2,1)S(1)}, u32[]{:S(2)}, u32[]{:S(2)}) %collective-permute-start.6) | collective-permute-done | bytes 131104 | tf_op jit(solution)/shard_map/ppermute | solution.py:17
  459.5 1.1 fusion.1
  460.7 1.3 copy.23
  (42 shorter events, 10.4 us)
Async XLA Ops:
  6.5 209.2 %copy-start = (bf16[1,128,4096]{2,1,0:T(8,128)(2,1)S(1)}, bf16[1,128,4096]{2,1,0:T(8,128)(2,1)}, u32[]{:S(2)}) copy-start(bf16[1,128,4096]{2,1,0:T(8,128)(2,1)} %param.5) | copy-start | bytes 3145732
  6.5 202.8 %all-gather.3.cloned.1.call-start = ((), (), s32[]{:S(2)}) async-start(), calls=%async_computation | async-start | bytes 4202496 | tf_op jit(solution)/shard_map/all_gather | solution.py:64
  7.3 400.1 %all-gather.5.cloned.1.call-start = ((), (), s32[]{:S(2)}) async-start(), calls=%async_computation.1 | async-start | bytes 4202496 | tf_op jit(solution)/shard_map/all_gather | solution.py:69
  14.2 0.7 copy-start.1
  410.5 10.9 %collective-permute-start.1 = (bf16[128,4,128]{0,2,1:T(8,128)(2,1)S(1)}, bf16[128,4,128]{0,2,1:T(8,128)(2,1)S(1)}, u32[]{:S(2)}, u32[]{:S(2)}) collective-permute-start(bf16[128,4,128]{0,2,1:T(8,128)(2,1)S(1)} %copy.15), channel_id=1, source_target_pairs={{0,1},{1,2},{2,3},{3,4},{4,5},{5,6},{6,7},{7,8},{8,9},{9,10},{10,1... | collective-permute-start | bytes 393224 | tf_op jit(solution)/shard_map/ppermute | solution.py:17
  413.8 10.6 %collective-permute-start = (bf16[128,4,128]{0,2,1:T(8,128)(2,1)S(1)}, bf16[128,4,128]{0,2,1:T(8,128)(2,1)S(1)}, u32[]{:S(2)}, u32[]{:S(2)}) collective-permute-start(bf16[128,4,128]{0,2,1:T(8,128)(2,1)S(1)} %pad_maximum_fusion.1), channel_id=1, source_target_pairs={{0,1},{1,2},{2,3},{3,4},{4,5},{5,6},{6,7},{7,8},{8,9},{9,10},{10,1... | collective-permute-start | bytes 393224 | tf_op jit(solution)/shard_map/ppermute | solution.py:17
  421.4 10.3 %collective-permute-start.3 = (bf16[128,4,128]{0,2,1:T(8,128)(2,1)S(1)}, bf16[128,4,128]{0,2,1:T(8,128)(2,1)S(1)}, u32[]{:S(2)}, u32[]{:S(2)}) collective-permute-start(bf16[128,4,128]{0,2,1:T(8,128)(2,1)S(1)} %collective-permute-done.1), channel_id=1, source_target_pairs={{0,1},{1,2},{2,3},{3,4},{4,5},{5,6},{6,7},{7,8},{8,9},{9,10},{10,1... | collective-permute-start | bytes 393224 | tf_op jit(solution)/shard_map/ppermute | solution.py:17
  424.4 10.2 %collective-permute-start.2 = (bf16[128,4,128]{0,2,1:T(8,128)(2,1)S(1)}, bf16[128,4,128]{0,2,1:T(8,128)(2,1)S(1)}, u32[]{:S(2)}, u32[]{:S(2)}) collective-permute-start(bf16[128,4,128]{0,2,1:T(8,128)(2,1)S(1)} %collective-permute-done), channel_id=1, source_target_pairs={{0,1},{1,2},{2,3},{3,4},{4,5},{5,6},{6,7},{7,8},{8,9},{9,10},{10,1... | collective-permute-start | bytes 393224 | tf_op jit(solution)/shard_map/ppermute | solution.py:17
  431.7 11.4 %collective-permute-start.5 = (bf16[128,4,128]{0,2,1:T(8,128)(2,1)S(1)}, bf16[128,4,128]{0,2,1:T(8,128)(2,1)S(1)}, u32[]{:S(2)}, u32[]{:S(2)}) collective-permute-start(bf16[128,4,128]{0,2,1:T(8,128)(2,1)S(1)} %collective-permute-done.3), channel_id=1, source_target_pairs={{0,1},{1,2},{2,3},{3,4},{4,5},{5,6},{6,7},{7,8},{8,9},{9,10},{10,1... | collective-permute-start | bytes 393224 | tf_op jit(solution)/shard_map/ppermute | solution.py:17
  434.6 10.4 %collective-permute-start.4 = (bf16[128,4,128]{0,2,1:T(8,128)(2,1)S(1)}, bf16[128,4,128]{0,2,1:T(8,128)(2,1)S(1)}, u32[]{:S(2)}, u32[]{:S(2)}) collective-permute-start(bf16[128,4,128]{0,2,1:T(8,128)(2,1)S(1)} %collective-permute-done.2), channel_id=1, source_target_pairs={{0,1},{1,2},{2,3},{3,4},{4,5},{5,6},{6,7},{7,8},{8,9},{9,10},{10,1... | collective-permute-start | bytes 393224 | tf_op jit(solution)/shard_map/ppermute | solution.py:17
  443.1 16.4 %collective-permute-start.7 = (bf16[128,4,128]{0,2,1:T(8,128)(2,1)S(1)}, bf16[128,4,128]{0,2,1:T(8,128)(2,1)S(1)}, u32[]{:S(2)}, u32[]{:S(2)}) collective-permute-start(bf16[128,4,128]{0,2,1:T(8,128)(2,1)S(1)} %collective-permute-done.5), channel_id=1, source_target_pairs={{0,1},{1,2},{2,3},{3,4},{4,5},{5,6},{6,7},{7,8},{8,9},{9,10},{10,1... | collective-permute-start | bytes 393224 | tf_op jit(solution)/shard_map/ppermute | solution.py:17
  445.0 10.2 %collective-permute-start.6 = (bf16[128,4,128]{0,2,1:T(8,128)(2,1)S(1)}, bf16[128,4,128]{0,2,1:T(8,128)(2,1)S(1)}, u32[]{:S(2)}, u32[]{:S(2)}) collective-permute-start(bf16[128,4,128]{0,2,1:T(8,128)(2,1)S(1)} %collective-permute-done.4), channel_id=1, source_target_pairs={{0,1},{1,2},{2,3},{3,4},{4,5},{5,6},{6,7},{7,8},{8,9},{9,10},{10,1... | collective-permute-start | bytes 393224 | tf_op jit(solution)/shard_map/ppermute | solution.py:17
Sparse Core Ops, SparseCore 0:
  11.9 197.3 all-gather.2
  213.9 193.3 all-gather.4
where the time goes:
time: 470 us; the launch traced here: 469 us
  waiting for transfers between devices  408 us (87%)
  starting transfers between devices  18.4 us (4%)
  between operations  13.7 us (3%)
  matrix products  11.9 us (3%)
  local copies, waits for them, and re-layouts  9.25 us (2%)
  other arithmetic  7.54 us (2%)
    all_gather x1, waiting for transfers between devices, shards(): lax.all_gather(key_weight, ('dp', 'ctx'), axis=0, tiled=True)  194 us
    all_gather x1, waiting for transfers between devices, shards(): lax.all_gather(value_weight, ('dp', 'ctx'), axis=0, tiled=True)  188 us
    ppermute x8, waiting for transfers between devices, shifted(): return lax.ppermute(block, axis, route)  24.2 us
    ppermute x8, starting transfers between devices, shifted(): return lax.ppermute(block, axis, route)  18.4 us
  transfers between devices with their start and end apart: 10, of which 8 were waited for; matrix products, arithmetic and copies ran while one was open for 5% of the time, Pallas kernels for 0%

commit v1 on v0

v1 whole, which is shorter than its diff:
```python
import functools
import math

import jax
import jax.numpy as jnp
from jax import lax
from jax.experimental import pallas as pl
from jax.experimental.pallas import tpu as pltpu
from jax.sharding import Mesh, PartitionSpec as P

HD = 128
NX, NC, NZ, NY = 4, 2, 16, 4
NEG_FILL = -1e30
BF16 = jnp.bfloat16
F32 = jnp.float32


def frequencies(head_size):
    halves = jnp.arange(head_size // 2, dtype=jnp.float32)
    base_rate = 500000.0 ** (-2.0 * halves / head_size)
    wavelength = 2.0 * math.pi / base_rate
    mixing = (8192.0 / wavelength - 1.0) / 3.0
    middle = (1.0 - mixing) * base_rate / 8.0 + mixing * base_rate
    return jnp.where(
        wavelength < 2048.0, base_rate, jnp.where(wavelength > 8192.0, base_rate / 8.0, middle)
    )


def positions(limits, places):
    return jnp.where(
        places < limits[2], places - limits[0], places - limits[0] - (limits[2] - limits[1])
    )


def cos_sin(offsets):
    angles = offsets[:, None] * frequencies(HD)[None, :]
    cos_part, sin_part = jnp.cos(angles), jnp.sin(angles)
    return (
        jnp.concatenate([cos_part, cos_part], axis=1),
        jnp.concatenate([-sin_part, sin_part], axis=1),
    )


def swap_halves(vectors):
    half = vectors.shape[-1] // 2
    return jnp.concatenate([vectors[..., half:], vectors[..., :half]], axis=-1)


def copies(block, count):
    return jnp.broadcast_to(block[None], (count,) + block.shape)


def project_kernel(core_ref, a_ref, b_ref, mine_ref, other_ref, cos_ref, sin_ref, out_ref, acc):
    step = pl.program_id(0)

    @pl.when(step == 0)
    def _():
        acc[...] = jnp.zeros_like(acc)

    acc[...] += jnp.dot(
        a_ref[...], mine_ref[0], preferred_element_type=F32
    ) + jnp.dot(b_ref[...], other_ref[0], preferred_element_type=F32)

    @pl.when(step == pl.num_programs(0) - 1)
    def _():
        keys = acc[:, :HD]
        out_ref[:, :HD] = (keys * cos_ref[...] + swap_halves(keys) * sin_ref[...]).astype(BF16)
        out_ref[:, HD:] = acc[:, HD:].astype(BF16)


def project(core, tokens, mine, other, cos, sin):
    rows = tokens.shape[0]
    depth = mine.shape[1]
    width = mine.shape[2]
    whole = lambda i, c: (0, 0)
    return pl.pallas_call(
        project_kernel,
        grid_spec=pltpu.PrefetchScalarGridSpec(
            num_scalar_prefetch=1,
            grid=(mine.shape[0],),
            in_specs=[
                pl.BlockSpec((rows, depth), lambda i, c: (0, 2 * i + c[0])),
                pl.BlockSpec((rows, depth), lambda i, c: (0, 2 * i + 1 - c[0])),
                pl.BlockSpec((1, depth, width), lambda i, c: (i, 0, 0)),
                pl.BlockSpec((1, depth, width), lambda i, c: (i, 0, 0)),
                pl.BlockSpec((rows, HD), whole),
                pl.BlockSpec((rows, HD), whole),
            ],
            out_specs=pl.BlockSpec((rows, width), whole),
            scratch_shapes=[pltpu.VMEM((rows, width), F32)],
        ),
        out_shape=jax.ShapeDtypeStruct((rows, width), BF16),
        compiler_params=pltpu.CompilerParams(vmem_limit_bytes=24 * 1024 * 1024),
        name="project",
    )(core, tokens, tokens, mine, other, cos, sin)


def attend_kernel(group, scale, q_ref, kv_ref, bias_ref, out_ref):
    keys = kv_ref[0, :, :HD]
    values = kv_ref[0, :, HD:]
    for head in range(group):
        cols = slice(head * HD, (head + 1) * HD)
        scores = lax.dot_general(
            q_ref[:, cols], keys, (((1,), (1,)), ((), ())), preferred_element_type=F32
        )
        scores = scores + bias_ref[...]
        highest = jnp.max(scores, axis=-1, keepdims=True)
        weights = jnp.exp2((scores - highest) * scale)
        totals = jnp.sum(weights, axis=-1, keepdims=True)
        context = jnp.dot(weights.astype(BF16), values, preferred_element_type=F32)
        out_ref[:, cols] = (context / totals).astype(BF16)


def attend(turned, window, bias):
    rows, width = turned.shape
    kv_heads, span, _ = window.shape
    per = width // kv_heads
    scale = HD ** (-0.5) * math.log2(math.e)
    return pl.pallas_call(
        functools.partial(attend_kernel, per // HD, scale),
        grid=(kv_heads,),
        in_specs=[
            pl.BlockSpec((rows, per), lambda g: (0, g)),
            pl.BlockSpec((1, span, 2 * HD), lambda g: (g, 0, 0)),
            pl.BlockSpec((rows, span), lambda g: (0, 0)),
        ],
        out_specs=pl.BlockSpec((rows, per), lambda g: (0, g)),
        out_shape=jax.ShapeDtypeStruct((rows, width), BF16),
        compiler_params=pltpu.CompilerParams(vmem_limit_bytes=24 * 1024 * 1024),
        name="attend",
    )(turned, window, bias)


def shards(tokens, queries, key_weight, value_weight, bounds):
    local_len = tokens.shape[1]
    features = tokens.shape[2]
    kv_heads = key_weight.shape[1] // HD
    rows = key_weight.shape[0]
    slab = NY * local_len
    y_at = lax.axis_index("y")
    core = lax.axis_index("core").astype(jnp.int32)
    my_index = lax.axis_index("z") * NY + y_at

    gathered = lax.all_to_all(copies(tokens[0], NY), "y", 0, 0).reshape(slab, features)

    places = my_index * local_len + jnp.arange(local_len, dtype=jnp.int32)
    limits = bounds[:, 0, :]
    offsets = positions(limits, places)

    by_head = jnp.concatenate(
        [
            key_weight.reshape(rows, kv_heads, HD),
            value_weight.reshape(rows, kv_heads, HD),
        ],
        axis=-1,
    ).transpose(1, 0, 2)
    coded = jnp.concatenate([offsets // 256, offsets % 256]).astype(BF16)
    parcel = jnp.concatenate(
        [by_head, jnp.broadcast_to(coded[None, None], (kv_heads, 8, 2 * HD))], axis=1
    )
    parcel = lax.all_to_all(parcel, "y", 0, 0)
    slab_code = parcel[:, rows, :].astype(F32)
    slab_offsets = (slab_code[:, :local_len] * 256.0 + slab_code[:, local_len:]).reshape(slab)
    weight = parcel[:, :rows, :].reshape(NY * rows, 2 * HD)
    weight = lax.all_to_all(copies(weight, NZ), "z", 0, 0).reshape(NZ * NY * rows, 2 * HD)
    weight = lax.all_to_all(copies(weight, NX), "x", 0, 0)
    other = lax.ppermute(weight, "core", [(0, 1), (1, 0)])

    cos, sin = cos_sin(slab_offsets)
    own_slab = project(core[None], gathered, weight, other, cos, sin)
    last_slab = lax.ppermute(own_slab, "z", [(i, i + 1) for i in range(NZ - 1)])
    span = slab + local_len
    both = jnp.concatenate([last_slab, own_slab], axis=0)
    windows = jnp.stack([both[i * local_len : i * local_len + span] for i in range(NY)])
    window = lax.all_to_all(windows, "y", 0, 0)

    own_cos, own_sin = cos_sin(offsets.astype(F32))
    raw = queries[0].astype(F32).reshape(local_len, -1, HD)
    turned = (raw * own_cos[:, None, :] + swap_halves(raw) * own_sin[:, None, :]).astype(BF16)
    turned = turned.reshape(local_len, -1)

    key_index = my_index * local_len - slab + jnp.arange(span, dtype=jnp.int32)
    begin_at, chosen_at, reject_at = (limits[i][:, None] for i in range(3))
    place = places[:, None]
    excluded = (place >= reject_at) & (key_index >= chosen_at) & (key_index < reject_at)
    visible = (key_index >= begin_at) & (key_index <= place) & jnp.logical_not(excluded)
    bias = jnp.where(visible, 0.0, NEG_FILL).astype(F32)

    return attend(turned, window, bias)[None]


def solution(mesh):
    fine = Mesh(mesh.devices.reshape(NX, NC, NZ, NY), ("x", "core", "z", "y"))
    dp, ctx = ("x", "core"), ("z", "y")
    return jax.shard_map(
        shards,
        mesh=fine,
        in_specs=(
            P(dp, ctx, None),
            P(dp, ctx, None),
            P(dp + ctx, None),
            P(dp + ctx, None),
            P(None, dp, ctx),
        ),
        out_specs=P(dp, ctx, None),
        check_vma=False,
    )
```

time: 470 us -> 153 us (0.33)
  the two profiles are of different devices: /device:TPU:134 before, /device:TPU:96 now
where the time goes in v1:
time: 153 us; the launch traced here: 152 us
  blocking collectives  56.6 us (37%)
  waiting for transfers between devices  47.4 us (31%)
  Pallas kernels  15.4 us (10%)
  starting transfers between devices  12.4 us (8%)
  other arithmetic  10.4 us (7%)
  local copies, waits for them, and re-layouts  9.71 us (6%)
    all_to_all x1, waiting for transfers between devices, shards(): lax.all_to_all(copies(tokens[0], NY), 'y', 0, 0).reshape(slab, features)  34.8 us
    all_to_all x1, blocking collectives, shards(): lax.all_to_all(copies(weight, NZ), 'z', 0, 0)  31 us
    all_to_all x1, blocking collectives, shards(): weight = lax.all_to_all(copies(weight, NX), 'x', 0, 0)  15.8 us
    pallas_call x1, Pallas kernels, attend(): pl.pallas_call(functools.partial(attend_kernel, per // HD, scale), grid=(...  11.2 us
    all_to_all x1, blocking collectives, shards(): parcel = lax.all_to_all(parcel, 'y', 0, 0)  9.71 us
    all_to_all x1, waiting for transfers between devices, shards(): window = lax.all_to_all(windows, 'y', 0, 0)  7.03 us
    all_to_all x1, starting transfers between devices, shards(): lax.all_to_all(copies(tokens[0], NY), 'y', 0, 0).reshape(slab, features)  4.99 us
    ppermute x1, waiting for transfers between devices, shards(): last_slab = lax.ppermute(own_slab, 'z', [(i, i + 1) for i in range(NZ - 1)])  4.37 us
  transfers between devices with their start and end apart: 4, of which 4 were waited for; matrix products, arithmetic and copies ran while one was open for 7% of the time, Pallas kernels for 0%

profile of v1, /device:TPU:96, one launch (start us, length us, event | category | flops | bytes accessed | tf_op | source)
XLA Modules:
  0.0 152.1 jit_solution(18094538018503739683)
XLA Ops:
  0.0 0.7 convert_bitcast_fusion.2
  0.7 0.7 maximum_bitcast_fusion
  1.5 9.7 %all_to_all.25 = bf16[4,16,256]{2,1,0:T(8,128)(2,1)S(1)} all-to-all(bf16[4,16,256]{2,1,0:T(8,128)(2,1)S(1)} %pad_maximum_fusion.6), channel_id=1, replica_groups=mesh['x'=4,'core'=2,'z'=16,'y'=4] {'y'}, dimensions={0} | all-to-all | bytes 65536 | tf_op jit(solution)/shard_map/all_to_all | solution.py:161
  11.2 31.0 %all_to_all.26 = bf16[16,32,256]{2,1,0:T(8,128)(2,1)S(1)} all-to-all(bf16[16,32,256]{2,1,0:T(8,128)(2,1)S(1)} %broadcast_in_dim.56), channel_id=1, replica_groups=mesh['x'=4,'core'=2,'z'=16,'y'=4] {'z'}, dimensions={0} | all-to-all | bytes 524288 | tf_op jit(solution)/shard_map/all_to_all | solution.py:165
  42.3 15.8 %all_to_all.27.mine_ref = bf16[4,512,256]{2,1,0:T(8,128)(2,1)S(1)} all-to-all(bf16[4,512,256]{2,1,0:T(8,128)(2,1)S(1)} %broadcast_in_dim.58), channel_id=1, replica_groups=mesh['x'=4,'core'=2,'z'=16,'y'=4] {'x'}, dimensions={0} | all-to-all | bytes 2097152 | tf_op jit(solution)/shard_map/all_to_all | solution.py:166
  58.2 2.5 %broadcast_in_dim.28 = bf16[4,128,4096]{2,1,0:T(8,128)(2,1)} broadcast(bf16[128,4096]{1,0:T(8,128)(2,1)S(1)} %bitcast.63), dimensions={1,2} | broadcast | bytes 5242880 | tf_op jit(solution)/shard_map/broadcast_in_dim | solution.py:50
  60.7 5.0 %all-to-all-start = ((bf16[4,128,4096]{2,1,0:T(8,128)(2,1)}), bf16[4,128,4096]{2,1,0:T(8,128)(2,1)}, u32[]{:S(2)}, u32[]{:S(2)}) async-start(bf16[4,128,4096]{2,1,0:T(8,128)(2,1)} %broadcast_in_dim.28), calls=%async_computation | async-start | bytes 8388608 | tf_op jit(solution)/shard_map/all_to_all | solution.py:144
  67.0 2.7 %fusion.17 = (f32[128,32,64]{2,1,0:T(8,128)}, f32[128,32,64]{2,1,0:T(8,128)}) fusion(f32[128,32,128]{2,1,0:T(8,128)S(1)} %bitcast.60), kind=kLoop, calls=%fused_computation.60 | loop fusion | bytes 4194304 | tf_op jit(solution)/shard_map/slice | solution.py:46
  69.7 1.9 %collective-permute-start = (bf16[4,512,256]{2,1,0:T(8,128)(2,1)S(1)}, bf16[4,512,256]{2,1,0:T(8,128)(2,1)S(1)}, u32[]{:S(2)}, u32[]{:S(2)}) collective-permute-start(bf16[4,512,256]{2,1,0:T(8,128)(2,1)S(1)} %all_to_all.27.mine_ref), channel_id=1, source_target_pairs={{0,64},{64,0},{1,65},{65,1},{2,66},{66,2},{3,67},{67,3},{4,68},{68... | collective-permute-start | bytes 3145736 | tf_op jit(solution)/shard_map/ppermute | solution.py:167
  71.9 1.0 fusion.10
  73.1 1.2 collective-permute-done.other_ref
  74.3 1.0 copy-done
  75.2 34.8 %all-to-all-done = bf16[4,128,4096]{2,1,0:T(8,128)(2,1)} async-done(((bf16[4,128,4096]{2,1,0:T(8,128)(2,1)}), bf16[4,128,4096]{2,1,0:T(8,128)(2,1)}, u32[]{:S(2)}, u32[]{:S(2)}) %all-to-all-start) | async-done | bytes 4194336 | tf_op jit(solution)/shard_map/all_to_all | solution.py:144
  110.1 1.2 copy-done.1
  111.3 4.2 %project.1 = bf16[512,256]{1,0:T(8,128)(2,1)S(1)} custom-call(s32[1]{0:T(128)} %bitcast.4.core_ref, bf16[512,4096]{1,0:T(8,128)(2,1)} %bitcast.6.a_ref.b_ref, bf16[512,4096]{1,0:T(8,128)(2,1)} %bitcast.6.a_ref.b_ref, bf16[4,512,256]{2,1,0:T(8,128)(2,1)S(1)} %all_to_all.27.mine_ref, bf16[4,512,256]{2,1,0:T(8,128)(2,1)S(1)} %copy-done.1, ...), custom_call_target="tpu_custom_call" | custom-call | tf_op jit(solution)/shard_map/project/pallas_call | solution.py:76
  115.5 1.9 %collective-permute-start.1 = (bf16[512,256]{1,0:T(8,128)(2,1)S(1)}, bf16[512,256]{1,0:T(8,128)(2,1)S(1)}, u32[]{:S(2)}, u32[]{:S(2)}) collective-permute-start(bf16[512,256]{1,0:T(8,128)(2,1)S(1)} %project.1), channel_id=1, source_target_pairs={{0,4},{4,8},{8,12},{12,16},{16,20},{20,24},{24,28},{28,32},{32,36}... | collective-permute-start | bytes 786440 | tf_op jit(solution)/shard_map/ppermute | solution.py:171
  117.4 1.9 %maximum_multiply_fusion = f32[128,32,128]{2,1,0:T(8,128)} fusion(f32[128,32,64]{2,1,0:T(8,128)S(1)} %copy-done.4, f32[128,32,64]{2,1,0:T(8,128)S(1)} %copy-done.3, f32[128,128]{1,0:T(8,128)S(1)} %get-tuple-element.23), kind=kLoop, calls=%fused_computation.5 | loop fusion | flops 1048576 | bytes 4259840 | tf_op jit(solution)/shard_map/mul | solution.py:179
  119.4 4.4 %collective-permute-done.1 = bf16[512,256]{1,0:T(8,128)(2,1)S(1)} collective-permute-done((bf16[512,256]{1,0:T(8,128)(2,1)S(1)}, bf16[512,256]{1,0:T(8,128)(2,1)S(1)}, u32[]{:S(2)}, u32[]{:S(2)}) %collective-permute-start.1) | collective-permute-done | bytes 262176 | tf_op jit(solution)/shard_map/ppermute | solution.py:171
  123.9 1.2 pad_maximum_fusion
  125.1 3.5 %all-to-all-start.4 = ((bf16[4,640,256]{2,1,0:T(8,128)(2,1)}), bf16[4,640,256]{2,1,0:T(8,128)(2,1)S(1)}, u32[]{:S(2)}, u32[]{:S(2)}) async-start(bf16[4,640,256]{2,1,0:T(8,128)(2,1)} %pad_maximum_fusion), calls=%async_computation.4 | async-start | bytes 2621440 | tf_op jit(solution)/shard_map/all_to_all | solution.py:175
  128.8 1.4 copy-done.2
  130.2 3.6 %fusion.2.q_ref = bf16[128,4096]{1,0:T(8,128)(2,1)S(1)} fusion(bf16[1,128,4096]{2,1,0:T(8,128)(2,1)} %param.6, f32[16,8,32,128]{3,2,1,0:T(8,128)S(1)} %bitcast.61, f32[16,8,32,128]{3,2,1,0:T(8,128)S(1)} %bitcast.62), kind=kLoop, calls=%fused_computation.4 | loop fusion | flops 2097152 | bytes 6291456 | tf_op jit(solution)/shard_map/convert_element_type | solution.py:179
  133.9 7.0 %all-to-all-done.4.kv_ref = bf16[4,640,256]{2,1,0:T(8,128)(2,1)S(1)} async-done(((bf16[4,640,256]{2,1,0:T(8,128)(2,1)}), bf16[4,640,256]{2,1,0:T(8,128)(2,1)S(1)}, u32[]{:S(2)}, u32[]{:S(2)}) %all-to-all-start.4) | async-done | bytes 1310752 | tf_op jit(solution)/shard_map/all_to_all | solution.py:175
  140.9 11.2 %attend.1 = bf16[128,4096]{1,0:T(8,128)(2,1)} custom-call(bf16[128,4096]{1,0:T(8,128)(2,1)S(1)} %fusion.2.q_ref, bf16[4,640,256]{2,1,0:T(8,128)(2,1)S(1)} %all-to-all-done.4.kv_ref, f32[128,640]{1,0:T(8,128)S(1)} %and_select_fusion.bias_ref), custom_call_target="tpu_custom_call" | custom-call | tf_op jit(solution)/shard_map/attend/pallas_call | solution.py:119
  (36 shorter events, 2.1 us)
Async XLA Ops:
  11.2 47.0 %copy-start.6 = (bf16[1,128,4096]{2,1,0:T(8,128)(2,1)S(1)}, bf16[1,128,4096]{2,1,0:T(8,128)(2,1)}, u32[]{:S(2)}) copy-start(bf16[1,128,4096]{2,1,0:T(8,128)(2,1)} %param.5) | copy-start | bytes 3145732
  60.7 5.0 %copy-start.5 = (bf16[1,128,4096]{2,1,0:T(8,128)(2,1)S(1)}, bf16[1,128,4096]{2,1,0:T(8,128)(2,1)}, u32[]{:S(2)}) copy-start(bf16[1,128,4096]{2,1,0:T(8,128)(2,1)} %param.6) | copy-start | bytes 3145732
  60.7 49.4 %all-to-all-start = ((bf16[4,128,4096]{2,1,0:T(8,128)(2,1)}), bf16[4,128,4096]{2,1,0:T(8,128)(2,1)}, u32[]{:S(2)}, u32[]{:S(2)}) async-start(bf16[4,128,4096]{2,1,0:T(8,128)(2,1)} %broadcast_in_dim.28), calls=%async_computation | async-start | bytes 8388608 | tf_op jit(solution)/shard_map/all_to_all | solution.py:144
  65.9 0.7 copy-start.7
  69.7 4.5 %collective-permute-start = (bf16[4,512,256]{2,1,0:T(8,128)(2,1)S(1)}, bf16[4,512,256]{2,1,0:T(8,128)(2,1)S(1)}, u32[]{:S(2)}, u32[]{:S(2)}) collective-permute-start(bf16[4,512,256]{2,1,0:T(8,128)(2,1)S(1)} %all_to_all.27.mine_ref), channel_id=1, source_target_pairs={{0,64},{64,0},{1,65},{65,1},{2,66},{66,2},{3,67},{67,3},{4,68},{68... | collective-permute-start | bytes 3145736 | tf_op jit(solution)/shard_map/ppermute | solution.py:167
  74.3 1.0 copy-start
  110.1 1.2 copy-start.1
  111.3 6.1 %copy-start.3 = (f32[128,32,64]{2,1,0:T(8,128)S(1)}, f32[128,32,64]{2,1,0:T(8,128)}, u32[]{:S(2)}) copy-start(f32[128,32,64]{2,1,0:T(8,128)} %get-tuple-element.7) | copy-start | bytes 3145732
  111.3 6.1 %copy-start.4 = (f32[128,32,64]{2,1,0:T(8,128)S(1)}, f32[128,32,64]{2,1,0:T(8,128)}, u32[]{:S(2)}) copy-start(f32[128,32,64]{2,1,0:T(8,128)} %get-tuple-element.8) | copy-start | bytes 3145732
  115.5 8.3 %collective-permute-start.1 = (bf16[512,256]{1,0:T(8,128)(2,1)S(1)}, bf16[512,256]{1,0:T(8,128)(2,1)S(1)}, u32[]{:S(2)}, u32[]{:S(2)}) collective-permute-start(bf16[512,256]{1,0:T(8,128)(2,1)S(1)} %project.1), channel_id=1, source_target_pairs={{0,4},{4,8},{8,12},{12,16},{16,20},{20,24},{24,28},{28,32},{32,36}... | collective-permute-start | bytes 786440 | tf_op jit(solution)/shard_map/ppermute | solution.py:171
  125.1 15.8 %all-to-all-start.4 = ((bf16[4,640,256]{2,1,0:T(8,128)(2,1)}), bf16[4,640,256]{2,1,0:T(8,128)(2,1)S(1)}, u32[]{:S(2)}, u32[]{:S(2)}) async-start(bf16[4,640,256]{2,1,0:T(8,128)(2,1)} %pad_maximum_fusion), calls=%async_computation.4 | async-start | bytes 2621440 | tf_op jit(solution)/shard_map/all_to_all | solution.py:175
  128.6 1.6 %copy-start.2 = (f32[128,32,128]{2,1,0:T(8,128)S(1)}, f32[128,32,128]{2,1,0:T(8,128)}, u32[]{:S(2)}) copy-start(f32[128,32,128]{2,1,0:T(8,128)} %maximum_multiply_fusion) | copy-start | bytes 6291460

commit v2 on v1

--- a/solution.py
+++ b/solution.py
@@ -95,37 +95,85 @@
     )(core, tokens, tokens, mine, other, cos, sin)
 
 
-def attend_kernel(group, scale, q_ref, kv_ref, bias_ref, out_ref):
-    keys = kv_ref[0, :, :HD]
-    values = kv_ref[0, :, HD:]
+def turn_kernel(group, q_ref, cos_ref, sin_ref, out_ref):
+    rows = q_ref.shape[0]
+    cos, sin = cos_ref[...], sin_ref[...]
     for head in range(group):
-        cols = slice(head * HD, (head + 1) * HD)
-        scores = lax.dot_general(
-            q_ref[:, cols], keys, (((1,), (1,)), ((), ())), preferred_element_type=F32
-        )
-        scores = scores + bias_ref[...]
-        highest = jnp.max(scores, axis=-1, keepdims=True)
-        weights = jnp.exp2((scores - highest) * scale)
-        totals = jnp.sum(weights, axis=-1, keepdims=True)
-        context = jnp.dot(weights.astype(BF16), values, preferred_element_type=F32)
-        out_ref[:, cols] = (context / totals).astype(BF16)
-
-
-def attend(turned, window, bias):
-    rows, width = turned.shape
-    kv_heads, span, _ = window.shape
+        raw = q_ref[:, head * HD : (head + 1) * HD].astype(F32)
+        turned = raw * cos + swap_halves(raw) * sin
+        out_ref[0, head * rows : (head + 1) * rows, :] = turned.astype(BF16)
+
+
+def turn(queries, cos, sin, kv_heads):
+    rows, width = queries.shape
     per = width // kv_heads
-    scale = HD ** (-0.5) * math.log2(math.e)
+    stacked = rows * per // HD
     return pl.pallas_call(
-        functools.partial(attend_kernel, per // HD, scale),
+        functools.partial(turn_kernel, per // HD),
         grid=(kv_heads,),
         in_specs=[
             pl.BlockSpec((rows, per), lambda g: (0, g)),
+            pl.BlockSpec((rows, HD), lambda g: (0, 0)),
+            pl.BlockSpec((rows, HD), lambda g: (0, 0)),
+        ],
+        out_specs=pl.BlockSpec((1, stacked, HD), lambda g: (g, 0, 0)),
+        out_shape=jax.ShapeDtypeStruct((kv_heads, stacked, HD), BF16),
+        compiler_params=pltpu.CompilerParams(vmem_limit_bytes=16 * 1024 * 1024),
+        name="turn",
+    )(queries, cos, sin)
+
+
+def attend_kernel(part, scale, q_ref, kv_ref, bias_ref, out_ref, left, right, paired):
+    rows = out_ref.shape[0]
+    stacked = q_ref.shape[1]
+    span = kv_ref.shape[1]
+
+    @pl.when(pl.program_id(0) == 0)
+    def _():
+        row = lax.broadcasted_iota(jnp.int32, (rows, rows), 0)
+        col = lax.broadcasted_iota(jnp.int32, (rows, rows), 1)
+        left[:, HD:] = jnp.where(row == col, 1.0, 0.0).astype(BF16)
+        right[HD:, :] = bias_ref[...]
+        paired[:, HD:] = jnp.ones((span, HD), BF16)
+
+    right[:HD, :] = kv_ref[0, :, :HD].T
+    paired[:, :HD] = kv_ref[0, :, HD:]
+    for first in range(0, stacked, part):
+        heads = [
+            jnp.concatenate([q_ref[0, at : at + rows, :], left[:, HD:]], axis=1)
+            for at in range(first, first + part, rows)
+        ]
+        block = jnp.concatenate(heads, axis=0)
+        scores = jnp.dot(block, right[...], preferred_element_type=F32)
+        highest = jnp.max(scores, axis=-1, keepdims=True)
+        weights = jnp.exp2((scores - highest) * scale).astype(BF16)
+        sums = jnp.dot(weights, paired[...], preferred_element_type=F32)
+        context = (sums[:, :HD] / sums[:, HD:]).astype(BF16)
+        for at in range(0, part, rows):
+            head = (first + at) // rows
+            out_ref[:, head * HD : (head + 1) * HD] = context[at : at + rows, :]
+
+
+def attend(turned, window, bias):
+    kv_heads, stacked, _ = turned.shape
+    rows, span = bias.shape
+    per = stacked // rows * HD
+    scale = HD ** (-0.5) * math.log2(math.e)
+    return pl.pallas_call(
+        functools.partial(attend_kernel, 2 * rows, scale),
+        grid=(kv_heads,),
+        in_specs=[
+            pl.BlockSpec((1, stacked, HD), lambda g: (g, 0, 0)),
             pl.BlockSpec((1, span, 2 * HD), lambda g: (g, 0, 0)),
             pl.BlockSpec((rows, span), lambda g: (0, 0)),
         ],
         out_specs=pl.BlockSpec((rows, per), lambda g: (0, g)),
-        out_shape=jax.ShapeDtypeStruct((rows, width), BF16),
+        out_shape=jax.ShapeDtypeStruct((rows, kv_heads * per), BF16),
+        scratch_shapes=[
+            pltpu.VMEM((rows, 2 * HD), BF16),
+            pltpu.VMEM((2 * HD, span), BF16),
+            pltpu.VMEM((span, 2 * HD), BF16),
+        ],
         compiler_params=pltpu.CompilerParams(vmem_limit_bytes=24 * 1024 * 1024),
         name="attend",
     )(turned, window, bias)
@@ -133,7 +181,6 @@
 
 def shards(tokens, queries, key_weight, value_weight, bounds):
     local_len = tokens.shape[1]
-    features = tokens.shape[2]
     kv_heads = key_weight.shape[1] // HD
     rows = key_weight.shape[0]
     slab = NY * local_len
@@ -141,7 +188,7 @@
     core = lax.axis_index("core").astype(jnp.int32)
     my_index = lax.axis_index("z") * NY + y_at
 
-    gathered = lax.all_to_all(copies(tokens[0], NY), "y", 0, 0).reshape(slab, features)
+    gathered = lax.all_gather(tokens[0], "y", axis=0, tiled=True)
 
     places = my_index * local_len + jnp.arange(local_len, dtype=jnp.int32)
     limits = bounds[:, 0, :]
@@ -175,16 +222,14 @@
     window = lax.all_to_all(windows, "y", 0, 0)
 
     own_cos, own_sin = cos_sin(offsets.astype(F32))
-    raw = queries[0].astype(F32).reshape(local_len, -1, HD)
-    turned = (raw * own_cos[:, None, :] + swap_halves(raw) * own_sin[:, None, :]).astype(BF16)
-    turned = turned.reshape(local_len, -1)
+    turned = turn(queries[0], own_cos, own_sin, kv_heads)
 
     key_index = my_index * local_len - slab + jnp.arange(span, dtype=jnp.int32)
     begin_at, chosen_at, reject_at = (limits[i][:, None] for i in range(3))
     place = places[:, None]
     excluded = (place >= reject_at) & (key_index >= chosen_at) & (key_index < reject_at)
     visible = (key_index >= begin_at) & (key_index <= place) & jnp.logical_not(excluded)
-    bias = jnp.where(visible, 0.0, NEG_FILL).astype(F32)
+    bias = jnp.where(visible, 0.0, NEG_FILL).astype(BF16)
 
     return attend(turned, window, bias)[None]
 

time: 153 us -> 122 us (0.80)
  the two profiles are of different devices: /device:TPU:96 before, /device:TPU:32 now
where the time goes in v2:
time: 122 us; the launch traced here: 121 us
  blocking collectives  57.4 us (47%)
  waiting for transfers between devices  25.9 us (21%)
  between operations  13.6 us (11%)
  Pallas kernels  9.53 us (8%)
  starting transfers between devices  8.11 us (7%)
  other arithmetic  4.68 us (4%)
  local copies, waits for them, and re-layouts  2.29 us (2%)
    all_to_all x1, blocking collectives, shards(): lax.all_to_all(copies(weight, NZ), 'z', 0, 0)  32.7 us
    all_to_all x1, waiting for transfers between devices, shards(): window = lax.all_to_all(windows, 'y', 0, 0)  16.1 us
    all_to_all x1, blocking collectives, shards(): weight = lax.all_to_all(copies(weight, NX), 'x', 0, 0)  15 us
    all_to_all x1, blocking collectives, shards(): parcel = lax.all_to_all(parcel, 'y', 0, 0)  9.71 us
    ppermute x1, waiting for transfers between devices, shards(): last_slab = lax.ppermute(own_slab, 'z', [(i, i + 1) for i in range(NZ - 1)])  7.68 us
    pallas_call x1, Pallas kernels, attend(): pl.pallas_call(functools.partial(attend_kernel, 2 * rows, scale), grid=(k...  6.4 us
    all_to_all x1, starting transfers between devices, shards(): window = lax.all_to_all(windows, 'y', 0, 0)  3.67 us
    ppermute x1, starting transfers between devices, shards(): last_slab = lax.ppermute(own_slab, 'z', [(i, i + 1) for i in range(NZ - 1)])  2.53 us
  transfers between devices with their start and end apart: 4, of which 3 were waited for; matrix products, arithmetic and copies ran while one was open for 3% of the time, Pallas kernels for 1%

profile of v2, /device:TPU:32, one launch (start us, length us, event | category | flops | bytes accessed | tf_op | source)
XLA Modules:
  0.0 121.5 jit_solution(3769005989649376946)
XLA Ops:
  6.5 0.7 all-gather.3.cloned.1.call-update
  7.3 0.7 convert_bitcast_fusion
  8.0 0.7 maximum_bitcast_fusion
  8.7 9.7 %all_to_all.20 = bf16[4,16,256]{2,1,0:T(8,128)(2,1)S(1)} all-to-all(bf16[4,16,256]{2,1,0:T(8,128)(2,1)S(1)} %pad_maximum_fusion.6), channel_id=1, replica_groups=mesh['x'=4,'core'=2,'z'=16,'y'=4] {'y'}, dimensions={0} | all-to-all | bytes 65536 | tf_op jit(solution)/shard_map/all_to_all | solution.py:208
  18.5 32.7 %all_to_all.21 = bf16[16,32,256]{2,1,0:T(8,128)(2,1)S(1)} all-to-all(bf16[16,32,256]{2,1,0:T(8,128)(2,1)S(1)} %broadcast_in_dim.45), channel_id=1, replica_groups=mesh['x'=4,'core'=2,'z'=16,'y'=4] {'z'}, dimensions={0} | all-to-all | bytes 524288 | tf_op jit(solution)/shard_map/all_to_all | solution.py:212
  51.2 0.1 broadcast_in_dim.47
  51.3 15.0 %all_to_all.22.mine_ref = bf16[4,512,256]{2,1,0:T(8,128)(2,1)S(1)} all-to-all(bf16[4,512,256]{2,1,0:T(8,128)(2,1)S(1)} %broadcast_in_dim.47), channel_id=1, replica_groups=mesh['x'=4,'core'=2,'z'=16,'y'=4] {'x'}, dimensions={0} | all-to-all | bytes 2097152 | tf_op jit(solution)/shard_map/all_to_all | solution.py:213
  66.3 1.9 %collective-permute-start = (bf16[4,512,256]{2,1,0:T(8,128)(2,1)S(1)}, bf16[4,512,256]{2,1,0:T(8,128)(2,1)S(1)}, u32[]{:S(2)}, u32[]{:S(2)}) collective-permute-start(bf16[4,512,256]{2,1,0:T(8,128)(2,1)S(1)} %all_to_all.22.mine_ref), channel_id=1, source_target_pairs={{0,64},{64,0},{1,65},{65,1},{2,66},{66,2},{3,67},{67,3},{4,68},{68... | collective-permute-start | bytes 3145736 | tf_op jit(solution)/shard_map/ppermute | solution.py:214
  68.3 1.0 fusion.7
  69.3 0.2 pad_maximum_fusion.2
  69.5 1.4 %collective-permute-done.other_ref = bf16[4,512,256]{2,1,0:T(8,128)(2,1)S(1)} collective-permute-done((bf16[4,512,256]{2,1,0:T(8,128)(2,1)S(1)}, bf16[4,512,256]{2,1,0:T(8,128)(2,1)S(1)}, u32[]{:S(2)}, u32[]{:S(2)}) %collective-permute-start) | collective-permute-done | bytes 1048608 | tf_op jit(solution)/shard_map/ppermute | solution.py:214
  70.8 2.2 %copy-done = bf16[1,512,4096]{2,1,0:T(8,128)(2,1)S(1)} copy-done((bf16[1,512,4096]{2,1,0:T(8,128)(2,1)S(1)}, bf16[1,512,4096]{2,1,0:T(8,128)(2,1)}, u32[]{:S(2)}) %copy-start) | copy-done | bytes 4194328
  73.0 2.3 %project.1 = bf16[512,256]{1,0:T(8,128)(2,1)S(1)} custom-call(s32[1]{0:T(128)} %bitcast.4.core_ref, bf16[512,4096]{1,0:T(8,128)(2,1)S(1)} %bitcast.42, bf16[512,4096]{1,0:T(8,128)(2,1)S(1)} %bitcast.43, bf16[4,512,256]{2,1,0:T(8,128)(2,1)S(1)} %all_to_all.22.mine_ref, bf16[4,512,256]{2,1,0:T(8,128)(2,1)S(1)} %collective-permute-done.other_ref, ...), custom_call_target="tpu_custom_call" | custom-call | tf_op jit(solution)/shard_map/project/pallas_call | solution.py:76
  75.4 2.5 %collective-permute-start.1 = (bf16[512,256]{1,0:T(8,128)(2,1)S(1)}, bf16[512,256]{1,0:T(8,128)(2,1)S(1)}, u32[]{:S(2)}, u32[]{:S(2)}) collective-permute-start(bf16[512,256]{1,0:T(8,128)(2,1)S(1)} %project.1), channel_id=1, source_target_pairs={{0,4},{4,8},{8,12},{12,16},{16,20},{20,24},{24,28},{28,32},{32,36}... | collective-permute-start | bytes 786440 | tf_op jit(solution)/shard_map/ppermute | solution.py:218
  77.9 7.7 %collective-permute-done.1 = bf16[512,256]{1,0:T(8,128)(2,1)S(1)} collective-permute-done((bf16[512,256]{1,0:T(8,128)(2,1)S(1)}, bf16[512,256]{1,0:T(8,128)(2,1)S(1)}, u32[]{:S(2)}, u32[]{:S(2)}) %collective-permute-start.1) | collective-permute-done | bytes 262176 | tf_op jit(solution)/shard_map/ppermute | solution.py:218
  85.6 0.1 fusion.3
  85.7 1.2 %pad_maximum_fusion = bf16[4,640,256]{2,1,0:T(8,128)(2,1)} fusion(bf16[1,640,256]{2,1,0:T(8,128)(2,1)S(1)} %get-tuple-element.9, bf16[1,640,256]{2,1,0:T(8,128)(2,1)S(1)} %get-tuple-element.10, bf16[1,640,256]{2,1,0:T(8,128)(2,1)S(1)} %get-tuple-element.8, bf16[1,640,256]{2,1,0:T(8,128)(2,1)S(1)} %get-tuple-element.7), kind=kLoop, calls=%fused_computation | loop fusion | flops 1966080 | bytes 2621440 | tf_op jit(solution)/shard_map/stack | solution.py:221
  86.9 3.7 %all-to-all-start.3 = ((bf16[4,640,256]{2,1,0:T(8,128)(2,1)}), bf16[4,640,256]{2,1,0:T(8,128)(2,1)S(1)}, u32[]{:S(2)}, u32[]{:S(2)}) async-start(bf16[4,640,256]{2,1,0:T(8,128)(2,1)} %pad_maximum_fusion), calls=%async_computation.3 | async-start | bytes 2621440 | tf_op jit(solution)/shard_map/all_to_all | solution.py:222
  90.6 0.3 fusion.8
  90.9 0.1 pad_maximum_fusion.4
  91.1 0.8 turn.1.q_ref
  91.9 0.2 select_convert_fusion.bias_ref
  92.1 16.1 %all-to-all-done.3.kv_ref = bf16[4,640,256]{2,1,0:T(8,128)(2,1)S(1)} async-done(((bf16[4,640,256]{2,1,0:T(8,128)(2,1)}), bf16[4,640,256]{2,1,0:T(8,128)(2,1)S(1)}, u32[]{:S(2)}, u32[]{:S(2)}) %all-to-all-start.3) | async-done | bytes 1310752 | tf_op jit(solution)/shard_map/all_to_all | solution.py:222
  108.2 6.4 %attend.1 = bf16[128,4096]{1,0:T(8,128)(2,1)} custom-call(bf16[4,1024,128]{2,1,0:T(8,128)(2,1)S(1)} %turn.1.q_ref, bf16[4,640,256]{2,1,0:T(8,128)(2,1)S(1)} %all-to-all-done.3.kv_ref, bf16[128,640]{1,0:T(8,128)(2,1)S(1)} %select_convert_fusion.bias_ref), custom_call_target="tpu_custom_call" | custom-call | tf_op jit(solution)/shard_map/attend/pallas_call | solution.py:162
  (21 shorter events, 0.1 us)
Async XLA Ops:
  6.5 64.3 %all-gather.3.cloned.1.call-start = ((), (), s32[]{:S(2)}) async-start(), calls=%async_computation.4 | async-start | bytes 5242880 | tf_op jit(solution)/shard_map/all_gather | solution.py:191
  66.3 4.5 %collective-permute-start = (bf16[4,512,256]{2,1,0:T(8,128)(2,1)S(1)}, bf16[4,512,256]{2,1,0:T(8,128)(2,1)S(1)}, u32[]{:S(2)}, u32[]{:S(2)}) collective-permute-start(bf16[4,512,256]{2,1,0:T(8,128)(2,1)S(1)} %all_to_all.22.mine_ref), channel_id=1, source_target_pairs={{0,64},{64,0},{1,65},{65,1},{2,66},{66,2},{3,67},{67,3},{4,68},{68... | collective-permute-start | bytes 3145736 | tf_op jit(solution)/shard_map/ppermute | solution.py:214
  70.8 2.2 %copy-start = (bf16[1,512,4096]{2,1,0:T(8,128)(2,1)S(1)}, bf16[1,512,4096]{2,1,0:T(8,128)(2,1)}, u32[]{:S(2)}) copy-start(bf16[1,512,4096]{2,1,0:T(8,128)(2,1)} %all-gather.3.cloned.1.call-done) | copy-start | bytes 12582916
  73.0 4.9 %copy-start.2 = (s32[3,1,128]{2,1,0:T(1,128)S(1)}, s32[3,1,128]{2,1,0:T(1,128)}, u32[]{:S(2)}) copy-start(s32[3,1,128]{2,1,0:T(1,128)} %param.9) | copy-start | bytes 4612
  75.4 10.2 %collective-permute-start.1 = (bf16[512,256]{1,0:T(8,128)(2,1)S(1)}, bf16[512,256]{1,0:T(8,128)(2,1)S(1)}, u32[]{:S(2)}, u32[]{:S(2)}) collective-permute-start(bf16[512,256]{1,0:T(8,128)(2,1)S(1)} %project.1), channel_id=1, source_target_pairs={{0,4},{4,8},{8,12},{12,16},{16,20},{20,24},{24,28},{28,32},{32,36}... | collective-permute-start | bytes 786440 | tf_op jit(solution)/shard_map/ppermute | solution.py:218
  86.9 4.1 %copy-start.1 = (bf16[1,128,4096]{2,1,0:T(8,128)(2,1)S(1)}, bf16[1,128,4096]{2,1,0:T(8,128)(2,1)}, u32[]{:S(2)}) copy-start(bf16[1,128,4096]{2,1,0:T(8,128)(2,1)} %param.6) | copy-start | bytes 3145732
  86.9 21.3 %all-to-all-start.3 = ((bf16[4,640,256]{2,1,0:T(8,128)(2,1)}), bf16[4,640,256]{2,1,0:T(8,128)(2,1)S(1)}, u32[]{:S(2)}, u32[]{:S(2)}) async-start(bf16[4,640,256]{2,1,0:T(8,128)(2,1)} %pad_maximum_fusion), calls=%async_computation.3 | async-start | bytes 2621440 | tf_op jit(solution)/shard_map/all_to_all | solution.py:222
Sparse Core Ops, SparseCore 0:
  9.5 60.0 all-gather.2
